TPU v7x, 32 devices: a whole 2x2x4 slice. The times are simulated.
32 devices in a mesh: gx: 8 (over z, y), gy: 4 (over x, core).
Axes of the slice: x: 2, y: 2, z: 4, core: 2. Of those that a mesh axis runs over, the one named last changes fastest.
Arguments:
- flux_perturbation: float32 [2, 4096, 4096], P(None, 'gx', 'gy'), may hold values from -6 to 6
- archived_nominal_heat_levels: float32 [2, 2, 4096, 4096], P(None, None, 'gx', 'gy'), may hold values from -4 to 4
- archived_solidity_labels: int32 [2, 2, 4096, 4096], P(None, None, 'gx', 'gy'), may hold values from 0 to 2
Outputs:
- hess_vec: float32 [2, 4096, 4096], P(None, 'gx', 'gy')
Inputs may be any that keep to these rules, and one draw needn't show every extreme that they name: `archived_solidity_labels`: 0 is solid, 1 mushy, 2 liquid.
All inputs are finite; a program needn't handle non-finite values.
Results may differ from a plain program's by a relative error of at most 0.000061.
Values sent between devices are 32-bit elements; how exact they have to be, the bound alone decides.
A program may use at most 192 MiB of HBM per device.

v0:
```python
import math
import jax
import jax.numpy as jnp
from jax import lax
from jax.sharding import PartitionSpec as P

TIME_STEP = 0.1
OBS_WEIGHT = 10.0
PRIOR_GAIN = 0.005
HIGHEST = lax.Precision.HIGHEST


def with_halo(cells, sides, width):
    for axis, dim in sides:
        count = lax.axis_size(axis)
        ends = count - 1
        head = lax.slice_in_dim(cells, 0, width, axis=dim)
        tail = lax.slice_in_dim(cells, cells.shape[dim] - width, cells.shape[dim], axis=dim)
        cells = jnp.concatenate(
            [
                lax.ppermute(tail, axis, [(i, (i + 1) % count) for i in range(ends)]),
                cells,
                lax.ppermute(head, axis, [((i + 1) % count, i) for i in range(ends)]),
            ],
            axis=dim,
        )
    return cells


def surface_rim(field):
    padded = with_halo(field, (("gx", 1), ("gy", 2)), 1)
    return padded[:, 2:, 1:-1] + padded[:, :-2, 1:-1] + padded[:, 1:-1, 2:] + padded[:, 1:-1, :-2]


def cos_sin(horizontal_line_total, col_count, modulus):
    row_ids = jnp.arange(horizontal_line_total, dtype=jnp.int32)[:, None]
    col_ids = jnp.arange(col_count, dtype=jnp.int32)[None, :]
    angles = (row_ids * col_ids % modulus).astype(jnp.float32) * (2.0 * math.pi / modulus)
    return (jnp.cos(angles), jnp.sin(angles))


def tables(length):
    bit_count = length.bit_length() - 1
    outer_len = 2 ** (bit_count // 2)
    inner_len = length // outer_len
    cos_outer, sin_outer = cos_sin(outer_len, outer_len, outer_len)
    cos_inner, sin_inner = cos_sin(inner_len, inner_len, inner_len)
    twist_cos, twist_sin = cos_sin(outer_len, inner_len, length)
    outer_fwd = jnp.stack([cos_outer, -sin_outer])
    inner_fwd = jnp.stack([jnp.stack([cos_inner, -sin_inner]), jnp.stack([sin_inner, cos_inner])])
    inner_inv = jnp.stack([jnp.stack([cos_inner, sin_inner]), jnp.stack([-sin_inner, cos_inner])])
    outer_inv = jnp.stack([cos_outer, -sin_outer])
    freq_index = (
        jnp.arange(outer_len, dtype=jnp.int32)[:, None]
        + outer_len * jnp.arange(inner_len, dtype=jnp.int32)[None, :]
    )
    signed = jnp.where(freq_index < length // 2, freq_index, freq_index - length).astype(
        jnp.float32
    )
    wave_sq = (signed * (2.0 * math.pi / length)) ** 2
    return (
        length,
        outer_len,
        inner_len,
        outer_fwd,
        inner_fwd,
        inner_inv,
        outer_inv,
        twist_cos,
        twist_sin,
        wave_sq,
    )


def forward(field, table):
    (
        length,
        outer_len,
        inner_len,
        outer_fwd,
        inner_fwd,
        inner_inv,
        outer_inv,
        twist_cos,
        twist_sin,
        wave_sq,
    ) = table
    grid = field.reshape(field.shape[:-1] + (outer_len, inner_len))
    stepped = jnp.einsum("...ab,rak->...rkb", grid, outer_fwd, precision=HIGHEST)
    step_re = stepped[..., 0, :, :]
    step_im = stepped[..., 1, :, :]
    twisted = jnp.stack(
        [step_re * twist_cos + step_im * twist_sin, step_im * twist_cos - step_re * twist_sin],
        axis=-3,
    )
    spec = jnp.einsum("...rkb,rsbm->...skm", twisted, inner_fwd, precision=HIGHEST)
    return (spec[..., 0, :, :], spec[..., 1, :, :])


def inverse(spec_re, spec_im, table):
    (
        length,
        outer_len,
        inner_len,
        outer_fwd,
        inner_fwd,
        inner_inv,
        outer_inv,
        twist_cos,
        twist_sin,
        wave_sq,
    ) = table
    stacked = jnp.stack([spec_re, spec_im], axis=-3)
    halved = jnp.einsum("...skm,srbm->...rkb", stacked, inner_inv, precision=HIGHEST)
    half_re = halved[..., 0, :, :]
    half_im = halved[..., 1, :, :]
    turned = jnp.stack(
        [half_re * twist_cos - half_im * twist_sin, half_im * twist_cos + half_re * twist_sin],
        axis=-3,
    )
    grid = jnp.einsum("...rkb,rka->...ab", turned, outer_inv, precision=HIGHEST)
    return grid.reshape(grid.shape[:-2] + (length,)) / length


def shards(flux_perturbation, archived_nominal_heat_levels, archived_solidity_labels):
    capacity = jnp.where(
        archived_solidity_labels == 0, 1.0, jnp.where(archived_solidity_labels == 1, 4.0, 1.25)
    ).astype(jnp.float32)
    diffusion_advance = jnp.where(
        archived_solidity_labels == 0, 1.0, jnp.where(archived_solidity_labels == 1, 0.6, 0.35)
    ).astype(jnp.float32)
    diffusion_advance = diffusion_advance * (1.0 + 0.5 * jnp.tanh(archived_nominal_heat_levels))
    rows = lax.all_to_all(flux_perturbation, "gx", split_axis=2, concat_axis=1, tiled=True)
    row_table = tables(rows.shape[1])
    first_u = TIME_STEP * flux_perturbation / capacity[0, 0]
    second_top = TIME_STEP * flux_perturbation + TIME_STEP * (
        diffusion_advance[0, 0] * (surface_rim(first_u) - 6.0 * first_u) + flux_perturbation
    )
    second_low = TIME_STEP * diffusion_advance[0, 1] * first_u
    top_u = second_top / capacity[1, 0]
    low_u = second_low / capacity[1, 1]
    third_top = second_top + TIME_STEP * (
        diffusion_advance[1, 0] * (surface_rim(top_u) - 6.0 * top_u + low_u) + flux_perturbation
    )
    misfit = OBS_WEIGHT * third_top / capacity[1, 0]
    adj_three = misfit / capacity[1, 0]
    push_top = TIME_STEP * diffusion_advance[1, 0] * adj_three
    adj_two_top = adj_three + (surface_rim(push_top) - 6.0 * push_top) / capacity[1, 0]
    adj_two_low = push_top / capacity[1, 1]
    pull_top = TIME_STEP * diffusion_advance[0, 0] * adj_two_top
    pull_low = TIME_STEP * diffusion_advance[0, 1] * adj_two_low
    adj_one_top = adj_two_top + (surface_rim(pull_top) - 6.0 * pull_top + pull_low) / capacity[0, 0]
    data_term = TIME_STEP * (adj_three + adj_two_top + adj_one_top)
    row_re, row_im = forward(jnp.swapaxes(rows, 1, 2), row_table)
    wave_x = row_table[-1]
    second_x = jnp.swapaxes(
        inverse(2.0 * PRIOR_GAIN * wave_x * row_re, 2.0 * PRIOR_GAIN * wave_x * row_im, row_table),
        1,
        2,
    )
    fourth_x = jnp.swapaxes(
        inverse(
            PRIOR_GAIN * wave_x * wave_x * row_re, PRIOR_GAIN * wave_x * wave_x * row_im, row_table
        ),
        1,
        2,
    )
    second_back, fourth_part = (
        lax.all_to_all(second_x, "gx", split_axis=1, concat_axis=2, tiled=True),
        lax.all_to_all(fourth_x, "gx", split_axis=1, concat_axis=2, tiled=True),
    )
    cols_dir, cols_second = (
        lax.all_to_all(flux_perturbation, "gy", split_axis=1, concat_axis=2, tiled=True),
        lax.all_to_all(second_back, "gy", split_axis=1, concat_axis=2, tiled=True),
    )
    col_table = tables(cols_dir.shape[2])
    dir_re, dir_im = forward(cols_dir, col_table)
    sec_re, sec_im = forward(cols_second, col_table)
    wave_y = col_table[-1]
    mixed = inverse(
        PRIOR_GAIN * wave_y * wave_y * dir_re + wave_y * sec_re,
        PRIOR_GAIN * wave_y * wave_y * dir_im + wave_y * sec_im,
        col_table,
    )
    mixed_back = lax.all_to_all(mixed, "gy", split_axis=2, concat_axis=1, tiled=True)
    return data_term + fourth_part + mixed_back


def solution(mesh):
    in_specs = (P(None, "gx", "gy"), P(None, None, "gx", "gy"), P(None, None, "gx", "gy"))
    out_specs = P(None, "gx", "gy")
    return jax.shard_map(shards, mesh=mesh, in_specs=in_specs, out_specs=out_specs, check_vma=False)
```

profile of v0, /device:TPU:17, one launch (start us, length us, event | category | flops | bytes accessed | tf_op | source)
XLA Modules:
  0.0 816.4 jit_solution(504303709747888213)
XLA Ops:
  0.0 7.4 copy.232
  7.4 5.5 all-to-all-start.2
  12.9 7.2 copy.218
  20.1 40.2 %all-to-all-done.2 = f32[2,512,1024]{2,0,1:T(2,128)} async-done(((f32[2,512,1024]{2,0,1:T(2,128)}), f32[2,512,1024]{2,0,1:T(2,128)}, u32[]{:S(2)}, u32[]{:S(2)}) %all-to-all-start.2) | async-done | bytes 4194336 | tf_op jit(solution)/shard_map/all_to_all | solution.py:173
  60.3 5.8 all-to-all-start
  67.5 5.6 copy.233
  73.1 5.3 copy.234
  78.5 13.3 %fusion.81 = f32[2,128,2,64,64]{1,3,4,0,2:T(8,128)} fusion(f32[2,128,64,64]{1,3,2,0:T(8,128)} %bitcast.223, f32[1,64,64]{1,2,0:T(8,128)S(1)} %get-tuple-element.69, f32[1,64,64]{1,2,0:T(8,128)S(1)} %get-tuple-element.70), kind=kOutput, calls=%fused_computation.149 | convolution fusion | flops 1610620928 | bytes 12615680 | tf_op jit(solution)/shard_map/...ab,rak->...rkb/dot_general | solution.py:89
  91.8 63.4 %all-to-all-done = f32[2,512,1024]{1,0,2:T(2,128)} async-done(((f32[2,512,1024]{1,0,2:T(2,128)}), f32[2,512,1024]{1,0,2:T(2,128)}, u32[]{:S(2)}, u32[]{:S(2)}) %all-to-all-start) | async-done | bytes 4194336 | tf_op jit(solution)/shard_map/all_to_all | solution.py:133
  155.2 5.0 copy.219
  160.2 5.4 copy.220
  165.6 11.7 %fusion.78 = f32[2,128,2,64,64]{1,3,4,0,2:T(8,128)S(1)} fusion(f32[2,128,64,64]{1,3,2,0:T(8,128)} %bitcast.224, f32[1,64,64]{1,2,0:T(8,128)S(1)} %get-tuple-element.69, f32[1,64,64]{1,2,0:T(8,128)S(1)} %get-tuple-element.70), kind=kOutput, calls=%fused_computation.148 | convolution fusion | flops 1610620928 | bytes 12615680 | tf_op jit(solution)/shard_map/...ab,rak->...rkb/dot_general | solution.py:89
  180.5 12.5 %fusion.87 = f32[2,128,2,64,64]{1,4,3,0,2:T(8,128)S(1)} fusion(f32[2,128,2,64,64]{1,3,4,0,2:T(8,128)S(1)} %pad_maximum_fusion, f32[1,2,64,64]{2,3,1,0:T(8,128)S(1)} %get-tuple-element.61, f32[1,2,64,64]{2,3,1,0:T(8,128)S(1)} %get-tuple-element.64), kind=kOutput, calls=%fused_computation.151 | convolution fusion | flops 3221241856 | bytes 16842752 | tf_op jit(solution)/shard_map/...rkb,rsbm->...skm/dot_general | solution.py:96
  193.1 3.5 slice_multiply_fusion.7
  196.6 8.5 %fusion.90 = f32[2,64,2,128,64]{3,1,4,2,0:T(8,128)S(1)} fusion(f32[2,128,1,64,64]{1,4,3,0,2:T(8,128)S(1)} %get-tuple-element.27, f32[2,128,1,64,64]{1,4,3,0,2:T(8,128)S(1)} %get-tuple-element.26, f32[1,2,64,64]{2,3,1,0:T(8,128)S(1)} %get-tuple-element.65, f32[1,2,64,64]{2,3,1,0:T(8,128)S(1)} %get-tuple-element.60), kind=kOutput, calls=%fused_computation.152 | convolution fusion | flops 3223339008 | bytes 16842752 | tf_op jit(solution)/shard_map/...skm,srbm->...rkb/dot_general | solution.py:114
  205.1 8.4 %copy.364 = f32[2,64,2,128,64]{3,4,1,2,0:T(8,128)} copy(f32[2,64,2,128,64]{3,1,4,2,0:T(8,128)S(1)} %fusion.90) | data formatting | bytes 16777216 | tf_op jit(solution)/shard_map/...skm,srbm->...rkb/dot_general | solution.py:114
  213.5 10.7 %fusion.96 = f32[2,64,2,128,64]{3,1,4,2,0:T(8,128)S(1)} fusion(f32[2,128,1,64,64]{1,4,3,0,2:T(8,128)S(1)} %get-tuple-element.38, f32[2,128,1,64,64]{1,4,3,0,2:T(8,128)} %get-tuple-element.39, f32[1,2,64,64]{2,3,1,0:T(8,128)S(1)} %get-tuple-element.65, f32[1,2,64,64]{2,3,1,0:T(8,128)S(1)} %get-tuple-element.60), kind=kOutput, calls=%fused_computation.154 | convolution fusion | flops 3223339008 | bytes 16842752 | tf_op jit(solution)/shard_map/...skm,srbm->...rkb/dot_general | solution.py:114
  224.2 8.5 %copy.363 = f32[2,64,2,128,64]{3,4,1,2,0:T(8,128)} copy(f32[2,64,2,128,64]{3,1,4,2,0:T(8,128)S(1)} %fusion.96) | data formatting | bytes 16777216 | tf_op jit(solution)/shard_map/...skm,srbm->...rkb/dot_general | solution.py:114
  232.7 12.8 %multiply_subtract_fusion.4 = (f32[2,128,1,64,64]{1,3,4,0,2:T(8,128)}, f32[2,128,1,64,64]{1,3,4,0,2:T(8,128)}, f32[2,128,1,64,64]{1,3,4,0,2:T(8,128)}, f32[2,128...) fusion(f32[2,128,2,64,64]{1,3,4,0,2:T(8,128)} %bitcast.221, ...), kind=kLoop, calls=%fused_computation.138 | loop fusion | flops 18874368 | bytes 50364416 | tf_op jit(solution)/shard_map/sub | solution.py:118
  245.6 4.9 fusion.66
  252.9 16.4 %copy.245 = f32[2,4096,128]{2,0,1:T(2,128)} copy(f32[2,4096,128]{2,1,0:T(8,128)S(1)} %bitcast.228) | data formatting | bytes 8388608 | tf_op jit(solution)/shard_map/transpose | solution.py:156
  269.3 8.0 all-to-all-start.3
  277.3 5.4 copy.181
  282.7 83.3 %all-to-all-done.3 = f32[2,4096,128]{2,0,1:T(2,128)} async-done(((f32[2,4096,128]{2,0,1:T(2,128)}), f32[2,4096,128]{2,0,1:T(2,128)}, u32[]{:S(2)}, u32[]{:S(2)}) %all-to-all-start.3) | async-done | bytes 4194336 | tf_op jit(solution)/shard_map/all_to_all | solution.py:169
  366.0 4.5 copy.246
  370.5 5.4 copy.247
  375.9 7.4 copy.248
  383.3 7.3 all-to-all-start.4
  390.5 9.8 %add_multiply_fusion = (f32[2,2,512,1024]{3,2,1,0:T(8,128)}, pred[2,2,512,1024]{3,2,1,0:T(8,128)(4,1)S(1)}, pred[2,2,512,1024]{3,2,1,0:T(8,128)(4,1)S(1)}) fusion(f32[2,2,512,1024]{3,2,1,0:T(8,128)} %param.4, s32[2,2,512,1024]{3,2,1,0:T(8,128)} %param.5), kind=kLoop, calls=%fused_computation.40 | loop fusion | flops 14680064 | bytes 29360128 | tf_op jit(solution)/shard_map/mul | solution.py:132
  423.1 7.3 fusion.67
  432.8 16.2 %copy.229 = f32[2,4096,128]{2,0,1:T(2,128)} copy(f32[2,4096,128]{2,1,0:T(8,128)S(1)} %bitcast.231) | data formatting | bytes 8388608 | tf_op jit(solution)/shard_map/transpose | solution.py:161
  449.0 8.1 all-to-all-start.1
  457.1 5.8 slice_bitcast_fusion.2
  466.9 4.4 collective-permute-start.3
  473.2 5.2 broadcast_multiply_fusion.3
  484.3 14.6 %broadcast_divide_fusion = f32[2,512,1024]{1,2,0:T(8,128)S(1)} fusion(f32[512,1024]{0,1:T(8,128)} %copy.192, f32[2,512,1024]{1,2,0:T(8,128)} %copy.181, f32[2,512,1024]{1,2,0:T(8,128)} %copy-done, f32[2,1,1024]{1,2,0:T(8,128)S(1)} %copy.185, f32[2,1,1024]{1,2,0:T(8,128)} %copy.187, f32[2,514,1]{1,2,0:T(1,128)S(1)} %collective-permute-done.3, ...), kind=kLoop, calls=%fused_computation.166 | loop fusion | flops 19922944 | bytes 16801824 | tf_op jit(solution)/shard_map/div | solution.py:140
  531.5 15.3 %collective-permute-done.4 = f32[2,1,1024]{2,0,1:T(2,128)} collective-permute-done((f32[2,1,1024]{2,0,1:T(2,128)}, f32[2,1,1024]{2,0,1:T(2,128)}, u32[]{:S(2)}, u32[]{:S(2)}) %collective-permute-start.4) | collective-permute-done | bytes 8224 | tf_op jit(solution)/shard_map/ppermute | solution.py:23
  553.2 4.1 collective-permute-start.7
  559.2 3.4 pad_maximum_fusion.2
  562.7 13.1 %fusion.93 = f32[2,128,2,64,64]{1,4,3,0,2:T(8,128)} fusion(f32[2,128,2,64,64]{1,3,4,0,2:T(8,128)S(1)} %pad_maximum_fusion.2, f32[1,2,64,64]{2,3,1,0:T(8,128)S(1)} %get-tuple-element.61, f32[1,2,64,64]{2,3,1,0:T(8,128)S(1)} %get-tuple-element.64), kind=kOutput, calls=%fused_computation.153 | convolution fusion | flops 3221241856 | bytes 16842752 | tf_op jit(solution)/shard_map/...rkb,rsbm->...skm/dot_general | solution.py:96
  575.7 5.5 copy.249
  581.3 5.4 copy.250
  586.6 11.3 %fusion.84 = f32[2,128,2,64,64]{1,3,4,0,2:T(8,128)S(1)} fusion(f32[2,128,64,64]{1,3,2,0:T(8,128)} %bitcast.225, f32[1,64,64]{1,2,0:T(8,128)S(1)} %get-tuple-element.69, f32[1,64,64]{1,2,0:T(8,128)S(1)} %get-tuple-element.70), kind=kOutput, calls=%fused_computation.150 | convolution fusion | flops 1610620928 | bytes 12615680 | tf_op jit(solution)/shard_map/...ab,rak->...rkb/dot_general | solution.py:89
  599.7 4.1 pad_maximum_fusion.4
  603.8 15.9 %fusion.99 = f32[2,128,2,64,64]{1,4,3,0,2:T(8,128)S(1)} fusion(f32[2,128,2,64,64]{1,3,4,0,2:T(8,128)} %pad_maximum_fusion.4, f32[1,2,64,64]{2,3,1,0:T(8,128)S(1)} %get-tuple-element.61, f32[1,2,64,64]{2,3,1,0:T(8,128)S(1)} %get-tuple-element.64), kind=kOutput, calls=%fused_computation.155 | convolution fusion | flops 3221241856 | bytes 16842752 | tf_op jit(solution)/shard_map/...rkb,rsbm->...skm/dot_general | solution.py:96
  619.8 4.7 fusion.31
  624.6 10.8 %fusion.102 = f32[2,64,2,128,64]{3,1,4,2,0:T(8,128)S(1)} fusion(f32[2,128,1,64,64]{1,4,3,0,2:T(8,128)} %get-tuple-element.13, f32[2,128,1,64,64]{1,4,3,0,2:T(8,128)} %get-tuple-element.12, f32[1,2,64,64]{2,3,1,0:T(8,128)S(1)} %get-tuple-element.65, f32[1,2,64,64]{2,3,1,0:T(8,128)S(1)} %get-tuple-element.60), kind=kOutput, calls=%fused_computation.156 | convolution fusion | flops 3223339008 | bytes 16842752 | tf_op jit(solution)/shard_map/...skm,srbm->...rkb/dot_general | solution.py:114
  635.4 4.9 copy.362
  642.2 4.9 fusion.65
  649.5 16.1 %copy.259 = f32[2,128,4096]{1,0,2:T(2,128)} copy(f32[2,128,4096]{1,2,0:T(8,128)S(1)} %bitcast.233) | data formatting | bytes 8388608 | tf_op jit(solution)/shard_map/div | solution.py:122
  665.7 5.0 all-to-all-start.5
  670.7 30.2 %broadcast_multiply_fusion.1 = (f32[2,512,1024]{1,2,0:T(8,128)S(1)}, f32[2,512,1024]{1,2,0:T(8,128)}) fusion(f32[512,1024]{0,1:T(8,128)} %copy.203, f32[512,1024]{0,1:T(8,128)} %copy.202, f32[2,512,1024]{1,2,0:T(8,128)} %copy.181, f32[512,1024]{0,1:T(8,128)} %copy.200, f32[512,1024]{0,1:T(8,128)S(1)} %copy.183, f32[512,1024]{0,1:T(8,128)} %copy.199, ...), kind=kLoop, calls=%fused_computation.165 | loop fusion | flops 44040192 | bytes 35700800 | tf_op jit(solution)/shard_map/mul | solution.py:147
  705.9 5.1 collective-permute-start.8
  718.9 5.1 collective-permute-start.11
  728.9 15.4 %broadcast_multiply_fusion = (f32[2,512,1024]{1,2,0:T(8,128)S(1)}, f32[2,512,1024]{1,2,0:T(8,128)}) fusion(f32[512,1024]{0,1:T(8,128)} %copy.210, f32[2,512,1024]{1,2,0:T(8,128)} %get-tuple-element.8, f32[512,1024]{0,1:T(8,128)} %copy.192, f32[2,512,1024]{1,2,0:T(8,128)} %copy-done.3, f32[2,1,1024]{1,2,0:T(8,128)S(1)} %copy.205, f32[2,1,1024]{1,2,0:T(8,128)} %copy.207, ...), kind=kLoop, calls=%fused_computation.164 | loop fusion | flops 16777216 | bytes 20996128 | tf_op jit(solution)/shard_map/mul | solution.py:150
  751.5 3.4 collective-permute-start.13
  759.0 4.7 collective-permute-start.15
  765.7 4.4 copy.230
  770.1 5.6 copy.231
  775.7 4.5 copy.260
  780.2 5.4 copy.261
  785.6 5.4 copy.262
  791.0 19.8 %fusion.72 = f32[2,512,1024]{1,2,0:T(8,128)} fusion(f32[2,512,1024]{1,2,0:T(8,128)} %copy.262, f32[2,512,8,128]{1,3,2,0:T(8,128)} %copy.231, f32[2,512,1024]{1,2,0:T(8,128)} %get-tuple-element.6, f32[2,512,1024]{1,2,0:T(8,128)} %copy-done.2, f32[2,1,1024]{1,2,0:T(8,128)S(1)} %copy.212, f32[2,1,1024]{1,2,0:T(8,128)} %copy.214, ...), kind=kLoop, calls=%fused_computation.123 | loop fusion | flops 25165824 | bytes 33579040 | tf_op jit(solution)/shard_map/add | solution.py:186
  810.8 5.4 copy.263
  (109 shorter events, 121.9 us)
Async XLA Ops:
  7.4 52.9 %all-to-all-start.2 = ((f32[2,512,1024]{2,0,1:T(2,128)}), f32[2,512,1024]{2,0,1:T(2,128)}, u32[]{:S(2)}, u32[]{:S(2)}) async-start(f32[2,512,1024]{2,0,1:T(2,128)} %copy.232), calls=%async_computation.2 | async-start | bytes 8388608 | tf_op jit(solution)/shard_map/all_to_all | solution.py:173
  60.3 94.9 %all-to-all-start = ((f32[2,512,1024]{1,0,2:T(2,128)}), f32[2,512,1024]{1,0,2:T(2,128)}, u32[]{:S(2)}, u32[]{:S(2)}) async-start(f32[2,512,1024]{1,0,2:T(2,128)} %copy.218), calls=%async_computation | async-start | bytes 8388608 | tf_op jit(solution)/shard_map/all_to_all | solution.py:133
  67.0 126.1 %copy-start.6 = (f32[64,64]{1,0:T(8,128)}, f32[64,64]{1,0:T(8,128)S(1)}, u32[]{:S(2)}) copy-start(f32[64,64]{1,0:T(8,128)S(1)} %copy.217) | copy-start | bytes 49156
  205.1 27.6 %slice-start.2 = ((s8[8388608]{0:T(1024)(128)(4,1)}), s8[4194304]{0:T(1024)(128)(4,1)S(1)}, s32[]{:S(2)}) async-start(s8[8388608]{0:T(1024)(128)(4,1)} %bitcast.219), calls=%async_computation.8 | async-start | bytes 8388608
  213.5 19.3 %slice-start.3 = ((s8[8388608]{0:T(1024)(128)(4,1)}), s8[4194304]{0:T(1024)(128)(4,1)S(1)}, s32[]{:S(2)}) async-start(s8[8388608]{0:T(1024)(128)(4,1)} %bitcast.219), calls=%async_computation.9 | async-start | bytes 8388608
  269.3 96.7 %all-to-all-start.3 = ((f32[2,4096,128]{2,0,1:T(2,128)}), f32[2,4096,128]{2,0,1:T(2,128)}, u32[]{:S(2)}, u32[]{:S(2)}) async-start(f32[2,4096,128]{2,0,1:T(2,128)} %copy.245), calls=%async_computation.3 | async-start | bytes 8388608 | tf_op jit(solution)/shard_map/all_to_all | solution.py:169
  383.3 65.7 %all-to-all-start.4 = ((f32[2,512,1024]{2,0,1:T(2,128)}), f32[2,512,1024]{2,0,1:T(2,128)}, u32[]{:S(2)}, u32[]{:S(2)}) async-start(f32[2,512,1024]{2,0,1:T(2,128)} %copy.248), calls=%async_computation.4 | async-start | bytes 8388608 | tf_op jit(solution)/shard_map/all_to_all | solution.py:174
  401.9 5.1 copy-start.4
  412.0 2.0 copy-start
  416.9 46.0 %collective-permute-start = (f32[2,1,1024]{2,0,1:T(2,128)S(1)}, f32[2,1,1024]{2,0,1:T(2,128)S(1)}, u32[]{:S(2)}, u32[]{:S(2)}) collective-permute-start(f32[2,1,1024]{2,0,1:T(2,128)S(1)} %copy.184), channel_id=1, source_target_pairs={{4,0},{8,4},{12,8},{16,12},{20,16},{24,20},{28,24},{5,1},{9,5},{13... | collective-permute-start | bytes 24584 | tf_op jit(solution)/shard_map/ppermute | solution.py:23
  420.9 42.4 %collective-permute-start.1 = (f32[2,1,1024]{2,0,1:T(2,128)}, f32[2,1,1024]{2,0,1:T(2,128)}, u32[]{:S(2)}, u32[]{:S(2)}) collective-permute-start(f32[2,1,1024]{2,0,1:T(2,128)} %copy.186), channel_id=1, source_target_pairs={{0,4},{4,8},{8,12},{12,16},{16,20},{20,24},{24,28},{1,5},{5,9},{9,... | collective-permute-start | bytes 24584 | tf_op jit(solution)/shard_map/ppermute | solution.py:21
  449.0 216.7 %all-to-all-start.1 = ((f32[2,4096,128]{2,0,1:T(2,128)}), f32[2,4096,128]{2,0,1:T(2,128)}, u32[]{:S(2)}, u32[]{:S(2)}) async-start(f32[2,4096,128]{2,0,1:T(2,128)} %copy.229), calls=%async_computation.1 | async-start | bytes 8388608 | tf_op jit(solution)/shard_map/all_to_all | solution.py:170
  466.9 17.4 %collective-permute-start.3 = (f32[2,514,1]{1,2,0:T(1,128)}, f32[2,514,1]{1,2,0:T(1,128)S(1)}, u32[]{:S(2)}, u32[]{:S(2)}) collective-permute-start(f32[2,514,1]{1,2,0:T(1,128)} %get-tuple-element.47), channel_id=1, source_target_pairs={{0,1},{1,2},{2,3},{4,5},{5,6},{6,7},{8,9},{9,10},{10,11},{12,13},{... | collective-permute-start | bytes 12344 | tf_op jit(solution)/shard_map/ppermute | solution.py:21
  471.2 13.0 %collective-permute-start.2 = (f32[2,514,1]{1,2,0:T(1,128)}, f32[2,514,1]{1,2,0:T(1,128)S(1)}, u32[]{:S(2)}, u32[]{:S(2)}) collective-permute-start(f32[2,514,1]{1,2,0:T(1,128)} %get-tuple-element.46), channel_id=1, source_target_pairs={{1,0},{2,1},{3,2},{5,4},{6,5},{7,6},{9,8},{10,9},{11,10},{13,12},{... | collective-permute-start | bytes 12344 | tf_op jit(solution)/shard_map/ppermute | solution.py:23
  498.9 2.1 copy-start.1
  504.8 42.1 %collective-permute-start.4 = (f32[2,1,1024]{2,0,1:T(2,128)}, f32[2,1,1024]{2,0,1:T(2,128)}, u32[]{:S(2)}, u32[]{:S(2)}) collective-permute-start(f32[2,1,1024]{2,0,1:T(2,128)} %copy.193), channel_id=1, source_target_pairs={{4,0},{8,4},{12,8},{16,12},{20,16},{24,20},{28,24},{5,1},{9,5},{13... | collective-permute-start | bytes 24584 | tf_op jit(solution)/shard_map/ppermute | solution.py:23
  510.0 39.5 %collective-permute-start.5 = (f32[2,1,1024]{2,0,1:T(2,128)}, f32[2,1,1024]{2,0,1:T(2,128)}, u32[]{:S(2)}, u32[]{:S(2)}) collective-permute-start(f32[2,1,1024]{2,0,1:T(2,128)} %copy.195), channel_id=1, source_target_pairs={{0,4},{4,8},{8,12},{12,16},{16,20},{20,24},{24,28},{1,5},{5,9},{9,... | collective-permute-start | bytes 24584 | tf_op jit(solution)/shard_map/ppermute | solution.py:21
  551.6 7.6 copy-start.5
  553.2 117.5 %collective-permute-start.7 = (f32[2,514,1]{1,2,0:T(1,128)}, f32[2,514,1]{1,2,0:T(1,128)}, u32[]{:S(2)}, u32[]{:S(2)}) collective-permute-start(f32[2,514,1]{1,2,0:T(1,128)} %get-tuple-element.45), channel_id=1, source_target_pairs={{0,1},{1,2},{2,3},{4,5},{5,6},{6,7},{8,9},{9,10},{10,11},{12,13},{... | collective-permute-start | bytes 12344 | tf_op jit(solution)/shard_map/ppermute | solution.py:21
  557.3 113.4 %collective-permute-start.6 = (f32[2,514,1]{1,2,0:T(1,128)}, f32[2,514,1]{1,2,0:T(1,128)}, u32[]{:S(2)}, u32[]{:S(2)}) collective-permute-start(f32[2,514,1]{1,2,0:T(1,128)} %get-tuple-element.44), channel_id=1, source_target_pairs={{1,0},{2,1},{3,2},{5,4},{6,5},{7,6},{9,8},{10,9},{11,10},{13,12},{... | collective-permute-start | bytes 12344 | tf_op jit(solution)/shard_map/ppermute | solution.py:23
  599.7 20.1 %slice-start = ((s8[8388608]{0:T(1024)(128)(4,1)}), s8[4194304]{0:T(1024)(128)(4,1)S(1)}, s32[]{:S(2)}) async-start(s8[8388608]{0:T(1024)(128)(4,1)} %bitcast.216), calls=%async_computation.6 | async-start | bytes 8388608
  603.8 16.0 %slice-start.1 = ((s8[8388608]{0:T(1024)(128)(4,1)}), s8[4194304]{0:T(1024)(128)(4,1)S(1)}, s32[]{:S(2)}) async-start(s8[8388608]{0:T(1024)(128)(4,1)} %bitcast.216), calls=%async_computation.7 | async-start | bytes 8388608
  603.8 16.0 %copy-start.7 = (f32[64,64]{1,0:T(8,128)S(1)}, f32[64,64]{1,0:T(8,128)}, u32[]{:S(2)}) copy-start(f32[64,64]{1,0:T(8,128)} %copy-done.6) | copy-start | bytes 49156
  603.8 16.0 %copy-start.8 = (f32[64,64]{1,0:T(8,128)S(1)}, f32[64,64]{1,0:T(8,128)}, u32[]{:S(2)}) copy-start(f32[64,64]{1,0:T(8,128)} %copy.238) | copy-start | bytes 49156
  665.7 110.1 %all-to-all-start.5 = ((f32[2,128,4096]{1,0,2:T(2,128)}), f32[2,128,4096]{1,0,2:T(2,128)}, u32[]{:S(2)}, u32[]{:S(2)}) async-start(f32[2,128,4096]{1,0,2:T(2,128)} %copy.259), calls=%async_computation.5 | async-start | bytes 8388608 | tf_op jit(solution)/shard_map/all_to_all | solution.py:185
  700.9 2.0 copy-start.3
  705.9 7.4 collective-permute-start.8
  711.3 5.3 collective-permute-start.9
  718.9 9.9 %collective-permute-start.11 = (f32[2,514,1]{1,2,0:T(1,128)S(1)}, f32[2,514,1]{1,2,0:T(1,128)S(1)}, u32[]{:S(2)}, u32[]{:S(2)}) collective-permute-start(f32[2,514,1]{1,2,0:T(1,128)S(1)} %get-tuple-element.43), channel_id=1, source_target_pairs={{0,1},{1,2},{2,3},{4,5},{5,6},{6,7},{8,9},{9,10},{10,11},{12,13},{... | collective-permute-start | bytes 12344 | tf_op jit(solution)/shard_map/ppermute | solution.py:21
  724.0 4.9 collective-permute-start.10
  744.3 2.0 copy-start.2
  749.2 5.6 collective-permute-start.12
  751.5 5.3 collective-permute-start.13
  759.0 31.9 %collective-permute-start.15 = (f32[2,514,1]{1,2,0:T(1,128)S(1)}, f32[2,514,1]{1,2,0:T(1,128)S(1)}, u32[]{:S(2)}, u32[]{:S(2)}) collective-permute-start(f32[2,514,1]{1,2,0:T(1,128)S(1)} %get-tuple-element.41), channel_id=1, source_target_pairs={{0,1},{1,2},{2,3},{4,5},{5,6},{6,7},{8,9},{9,10},{10,11},{12,13},{... | collective-permute-start | bytes 12344 | tf_op jit(solution)/shard_map/ppermute | solution.py:21
  763.7 27.2 %collective-permute-start.14 = (f32[2,514,1]{1,2,0:T(1,128)S(1)}, f32[2,514,1]{1,2,0:T(1,128)S(1)}, u32[]{:S(2)}, u32[]{:S(2)}) collective-permute-start(f32[2,514,1]{1,2,0:T(1,128)S(1)} %get-tuple-element.40), channel_id=1, source_target_pairs={{1,0},{2,1},{3,2},{5,4},{6,5},{7,6},{9,8},{10,9},{11,10},{13,12},{... | collective-permute-start | bytes 12344 | tf_op jit(solution)/shard_map/ppermute | solution.py:23
where the time goes:
time: 823 us; the launch traced here: 816 us
  local copies, waits for them, and re-layouts  244 us (30%)
  waiting for transfers between devices  208 us (25%)
  other arithmetic  150 us (18%)
  matrix products  125 us (15%)
  starting transfers between devices  88.5 us (11%)
    all_to_all x1, waiting for transfers between devices, shards(): lax.all_to_all(second_x, 'gx', split_axis=1, concat_axis=2, tiled=True)  83.3 us
    all_to_all x1, waiting for transfers between devices, shards(): lax.all_to_all(flux_perturbation, 'gx', split_axis=2, concat_axis=1, tile...  63.4 us
    dot_general x3, matrix products, forward(): jnp.einsum('...rkb,rsbm->...skm', twisted, inner_fwd, precision=HIGHEST)  41.5 us
    all_to_all x1, waiting for transfers between devices, shards(): lax.all_to_all(flux_perturbation, 'gy', split_axis=1, concat_axis=2, tile...  40.2 us
    dot_general x3, matrix products, forward(): jnp.einsum('...ab,rak->...rkb', grid, outer_fwd, precision=HIGHEST)  36.2 us
    mul x2, other arithmetic, shards(): push_top = TIME_STEP * diffusion_advance[1, 0] * adj_three  35.4 us
    unnamed x29, local copies, waits for them, and re-layouts  30.3 us
    dot_general x3, matrix products, inverse(): jnp.einsum('...skm,srbm->...rkb', stacked, inner_inv, precision=HIGHEST)  30 us
  transfers between devices with their start and end apart: 22, of which 8 were waited for; matrix products, arithmetic and copies ran while one was open for 42% of the time, Pallas kernels for 0%

commit v1 on v0

--- a/solution.py
+++ b/solution.py
@@ -8,6 +8,28 @@
 OBS_WEIGHT = 10.0
 PRIOR_GAIN = 0.005
 HIGHEST = lax.Precision.HIGHEST
+
+
+def in_blocks(shard, dim, length):
+    before, after = (shard.shape[:dim], shard.shape[dim + 1 :])
+    return jnp.moveaxis(shard.reshape(*before, length, -1, *after), dim, 0)
+
+
+def joined_along(blocks, dim):
+    lengths = list(blocks.shape[1:])
+    lengths[dim] *= blocks.shape[0]
+    return jnp.moveaxis(blocks, 0, dim).reshape(lengths)
+
+
+def exchange_in_pairs(x, axis, split_dim, concat_dim):
+    peers, index = (lax.axis_size(axis), lax.axis_index(axis))
+    blocks = in_blocks(x, split_dim, peers)
+    done = [blocks[index]]
+    for step in range(1, peers):
+        sent = blocks[index ^ step]
+        done.append(lax.ppermute(sent, axis, [(i, i ^ step) for i in range(peers)]))
+    blocks = jnp.stack(done)[index ^ jnp.arange(peers)]
+    return joined_along(blocks, concat_dim)
 
 
 def with_halo(cells, sides, width):
@@ -170,7 +192,7 @@
         lax.all_to_all(fourth_x, "gx", split_axis=1, concat_axis=2, tiled=True),
     )
     cols_dir, cols_second = (
-        lax.all_to_all(flux_perturbation, "gy", split_axis=1, concat_axis=2, tiled=True),
+        exchange_in_pairs(flux_perturbation, "gy", 1, 2),
         lax.all_to_all(second_back, "gy", split_axis=1, concat_axis=2, tiled=True),
     )
     col_table = tables(cols_dir.shape[2])

time: 823 us -> 771 us (0.937)
  waiting for transfers between devices: 208 us -> 156 us
    all_to_all x1, waiting for transfers between devices: 63.4 us -> 8.69 us  [shards(): lax.all_to_all(flux_perturbation, 'gx', split_axis=2, concat_axis=1, tile...]
    ppermute x0 -> x3, waiting for transfers between devices: none -> 43.7 us  [exchange_in_pairs(): done.append(lax.ppermute(sent, axis, [(i, i ^ step) for i in range(peers)]))]
    all_to_all x1 -> x0, waiting for transfers between devices: 40.2 us -> none  [shards(): lax.all_to_all(flux_perturbation, 'gy', split_axis=1, concat_axis=2, tile...]
    all_to_all x2 -> x0, local copies, waits for them, and re-layouts: 10.9 us -> none  [shards(): lax.all_to_all(flux_perturbation, 'gy', split_axis=1, concat_axis=2, tile...]
    unnamed x29 -> x30, local copies, waits for them, and re-layouts: 30.3 us -> 22.7 us
  transfers between devices with their start and end apart: 22 -> 24, of which waited for: 8 -> 9; matrix products, arithmetic and copies ran while one was open for 42% -> 45% of each run, Pallas kernels for 0% -> 0%
where the time goes in v1:
time: 771 us; the launch traced here: 762 us
  local copies, waits for them, and re-layouts  241 us (31%)
  waiting for transfers between devices  156 us (20%)
  other arithmetic  154 us (20%)
  matrix products  125 us (16%)
  starting transfers between devices  85.3 us (11%)
    all_to_all x1, waiting for transfers between devices, shards(): lax.all_to_all(second_x, 'gx', split_axis=1, concat_axis=2, tiled=True)  83.3 us
    ppermute x3, waiting for transfers between devices, exchange_in_pairs(): done.append(lax.ppermute(sent, axis, [(i, i ^ step) for i in range(peers)]))  43.7 us
    dot_general x3, matrix products, forward(): jnp.einsum('...rkb,rsbm->...skm', twisted, inner_fwd, precision=HIGHEST)  42 us
    dot_general x3, matrix products, forward(): jnp.einsum('...ab,rak->...rkb', grid, outer_fwd, precision=HIGHEST)  36 us
    mul x2, other arithmetic, shards(): push_top = TIME_STEP * diffusion_advance[1, 0] * adj_three  35.1 us
    dot_general x3, matrix products, inverse(): jnp.einsum('...skm,srbm->...rkb', stacked, inner_inv, precision=HIGHEST)  29.8 us
    ppermute x8, starting transfers between devices, with_halo(): lax.ppermute(tail, axis, [(i, (i + 1) % count) for i in range(ends)])  27.9 us
    div x4, local copies, waits for them, and re-layouts, inverse(): return grid.reshape(grid.shape[:-2] + (length,)) / length  23.4 us
  transfers between devices with their start and end apart: 24, of which 9 were waited for; matrix products, arithmetic and copies ran while one was open for 45% of the time, Pallas kernels for 0%

profile of v1, /device:TPU:17, one launch (start us, length us, event | category | flops | bytes accessed | tf_op | source)
XLA Modules:
  0.0 761.9 jit_solution(8609543655886416063)
XLA Ops:
  0.0 7.2 copy.224
  7.2 5.6 all-to-all-start
  12.8 3.5 dynamic-slice_bitcast_fusion.3
  21.7 21.3 %collective-permute-done.18 = f32[2,128,1024]{2,1,0:T(8,128)} collective-permute-done((f32[2,128,1024]{2,1,0:T(8,128)}, f32[2,128,1024]{2,1,0:T(8,128)}, u32[]{:S(2)}, u32[]{:S(2)}) %collective-permute-start.18) | collective-permute-done | bytes 1048608 | tf_op jit(solution)/shard_map/ppermute | solution.py:30
  43.0 22.4 %collective-permute-done.17 = f32[2,128,1024]{2,1,0:T(8,128)} collective-permute-done((f32[2,128,1024]{2,1,0:T(8,128)S(1)}, f32[2,128,1024]{2,1,0:T(8,128)}, u32[]{:S(2)}, u32[]{:S(2)}) %collective-permute-start.17) | collective-permute-done | bytes 1048608 | tf_op jit(solution)/shard_map/ppermute | solution.py:30
  65.4 4.5 pad_maximum_fusion.38
  69.9 4.9 gather_fusion
  74.8 5.3 copy.242
  80.1 13.3 %fusion.81 = f32[2,128,2,64,64]{1,3,4,0,2:T(8,128)} fusion(f32[2,128,64,64]{1,3,2,0:T(8,128)} %bitcast.244, f32[1,64,64]{1,2,0:T(8,128)S(1)} %get-tuple-element.73, f32[1,64,64]{1,2,0:T(8,128)S(1)} %get-tuple-element.74), kind=kOutput, calls=%fused_computation.151 | convolution fusion | flops 1610620928 | bytes 12615680 | tf_op jit(solution)/shard_map/...ab,rak->...rkb/dot_general | solution.py:111
  93.4 8.7 %all-to-all-done = f32[2,512,1024]{1,0,2:T(2,128)} async-done(((f32[2,512,1024]{1,0,2:T(2,128)}), f32[2,512,1024]{1,0,2:T(2,128)}, u32[]{:S(2)}, u32[]{:S(2)}) %all-to-all-start) | async-done | bytes 4194336 | tf_op jit(solution)/shard_map/all_to_all | solution.py:155
  102.1 5.0 copy.225
  107.2 5.4 copy.226
  112.5 11.4 %fusion.78 = f32[2,128,2,64,64]{1,3,4,0,2:T(8,128)S(1)} fusion(f32[2,128,64,64]{1,3,2,0:T(8,128)} %bitcast.245, f32[1,64,64]{1,2,0:T(8,128)S(1)} %get-tuple-element.73, f32[1,64,64]{1,2,0:T(8,128)S(1)} %get-tuple-element.74), kind=kOutput, calls=%fused_computation.150 | convolution fusion | flops 1610620928 | bytes 12615680 | tf_op jit(solution)/shard_map/...ab,rak->...rkb/dot_general | solution.py:111
  127.2 12.8 %fusion.87 = f32[2,128,2,64,64]{1,4,3,0,2:T(8,128)S(1)} fusion(f32[2,128,2,64,64]{1,3,4,0,2:T(8,128)S(1)} %pad_maximum_fusion, f32[1,2,64,64]{2,3,1,0:T(8,128)S(1)} %get-tuple-element.65, f32[1,2,64,64]{2,3,1,0:T(8,128)S(1)} %get-tuple-element.68), kind=kOutput, calls=%fused_computation.153 | convolution fusion | flops 3221241856 | bytes 16842752 | tf_op jit(solution)/shard_map/...rkb,rsbm->...skm/dot_general | solution.py:118
  140.0 3.5 slice_multiply_fusion.7
  143.5 8.5 %fusion.90 = f32[2,64,2,128,64]{3,1,4,2,0:T(8,128)S(1)} fusion(f32[2,128,1,64,64]{1,4,3,0,2:T(8,128)S(1)} %get-tuple-element.27, f32[2,128,1,64,64]{1,4,3,0,2:T(8,128)S(1)} %get-tuple-element.26, f32[1,2,64,64]{2,3,1,0:T(8,128)S(1)} %get-tuple-element.69, f32[1,2,64,64]{2,3,1,0:T(8,128)S(1)} %get-tuple-element.64), kind=kOutput, calls=%fused_computation.154 | convolution fusion | flops 3223339008 | bytes 16842752 | tf_op jit(solution)/shard_map/...skm,srbm->...rkb/dot_general | solution.py:136
  152.0 8.4 %copy.376 = f32[2,64,2,128,64]{3,4,1,2,0:T(8,128)} copy(f32[2,64,2,128,64]{3,1,4,2,0:T(8,128)S(1)} %fusion.90) | data formatting | bytes 16777216 | tf_op jit(solution)/shard_map/...skm,srbm->...rkb/dot_general | solution.py:136
  160.4 10.7 %fusion.96 = f32[2,64,2,128,64]{3,1,4,2,0:T(8,128)S(1)} fusion(f32[2,128,1,64,64]{1,4,3,0,2:T(8,128)S(1)} %get-tuple-element.38, f32[2,128,1,64,64]{1,4,3,0,2:T(8,128)} %get-tuple-element.39, f32[1,2,64,64]{2,3,1,0:T(8,128)S(1)} %get-tuple-element.69, f32[1,2,64,64]{2,3,1,0:T(8,128)S(1)} %get-tuple-element.64), kind=kOutput, calls=%fused_computation.156 | convolution fusion | flops 3223339008 | bytes 16842752 | tf_op jit(solution)/shard_map/...skm,srbm->...rkb/dot_general | solution.py:136
  171.1 8.3 %copy.375 = f32[2,64,2,128,64]{3,4,1,2,0:T(8,128)} copy(f32[2,64,2,128,64]{3,1,4,2,0:T(8,128)S(1)} %fusion.96) | data formatting | bytes 16777216 | tf_op jit(solution)/shard_map/...skm,srbm->...rkb/dot_general | solution.py:136
  179.5 12.8 %multiply_subtract_fusion.4 = (f32[2,128,1,64,64]{1,3,4,0,2:T(8,128)}, f32[2,128,1,64,64]{1,3,4,0,2:T(8,128)}, f32[2,128,1,64,64]{1,3,4,0,2:T(8,128)}, f32[2,128...) fusion(f32[2,128,2,64,64]{1,3,4,0,2:T(8,128)} %bitcast.242, ...), kind=kLoop, calls=%fused_computation.140 | loop fusion | flops 18874368 | bytes 50364416 | tf_op jit(solution)/shard_map/sub | solution.py:140
  192.3 4.9 fusion.66
  199.6 16.7 %copy.253 = f32[2,4096,128]{2,0,1:T(2,128)} copy(f32[2,4096,128]{2,1,0:T(8,128)S(1)} %bitcast.249) | data formatting | bytes 8388608 | tf_op jit(solution)/shard_map/transpose | solution.py:178
  216.3 7.8 %all-to-all-start.2 = ((f32[2,4096,128]{2,0,1:T(2,128)}), f32[2,4096,128]{2,0,1:T(2,128)}, u32[]{:S(2)}, u32[]{:S(2)}) async-start(f32[2,4096,128]{2,0,1:T(2,128)} %copy.253), calls=%async_computation.2 | async-start | bytes 8388608 | tf_op jit(solution)/shard_map/all_to_all | solution.py:191
  224.1 5.4 copy.187
  229.5 83.3 %all-to-all-done.2 = f32[2,4096,128]{2,0,1:T(2,128)} async-done(((f32[2,4096,128]{2,0,1:T(2,128)}), f32[2,4096,128]{2,0,1:T(2,128)}, u32[]{:S(2)}, u32[]{:S(2)}) %all-to-all-start.2) | async-done | bytes 4194336 | tf_op jit(solution)/shard_map/all_to_all | solution.py:191
  312.8 4.5 copy.254
  317.2 5.4 copy.255
  322.6 7.4 copy.256
  330.1 7.3 all-to-all-start.3
  337.3 9.8 %add_multiply_fusion = (f32[2,2,512,1024]{3,2,1,0:T(8,128)}, pred[2,2,512,1024]{3,2,1,0:T(8,128)(4,1)S(1)}, pred[2,2,512,1024]{3,2,1,0:T(8,128)(4,1)S(1)}) fusion(f32[2,2,512,1024]{3,2,1,0:T(8,128)} %param.4, s32[2,2,512,1024]{3,2,1,0:T(8,128)} %param.5), kind=kLoop, calls=%fused_computation.41 | loop fusion | flops 14680064 | bytes 29360128 | tf_op jit(solution)/shard_map/mul | solution.py:154
  369.9 7.1 fusion.67
  379.4 16.2 %copy.235 = f32[2,4096,128]{2,0,1:T(2,128)} copy(f32[2,4096,128]{2,1,0:T(8,128)S(1)} %bitcast.252) | data formatting | bytes 8388608 | tf_op jit(solution)/shard_map/transpose | solution.py:183
  395.6 8.1 %all-to-all-start.1 = ((f32[2,4096,128]{2,0,1:T(2,128)}), f32[2,4096,128]{2,0,1:T(2,128)}, u32[]{:S(2)}, u32[]{:S(2)}) async-start(f32[2,4096,128]{2,0,1:T(2,128)} %copy.235), calls=%async_computation.1 | async-start | bytes 8388608 | tf_op jit(solution)/shard_map/all_to_all | solution.py:192
  403.7 6.0 slice_bitcast_fusion.2
  413.6 4.4 collective-permute-start.3
  419.9 5.2 broadcast_multiply_fusion.3
  431.1 14.5 %broadcast_divide_fusion = f32[2,512,1024]{1,2,0:T(8,128)S(1)} fusion(f32[512,1024]{0,1:T(8,128)} %copy.198, f32[2,512,1024]{1,2,0:T(8,128)} %copy.187, f32[2,512,1024]{1,2,0:T(8,128)} %copy-done, f32[2,1,1024]{1,2,0:T(8,128)S(1)} %copy.191, f32[2,1,1024]{1,2,0:T(8,128)} %copy.193, f32[2,514,1]{1,2,0:T(1,128)S(1)} %collective-permute-done.3, ...), kind=kLoop, calls=%fused_computation.168 | loop fusion | flops 19922944 | bytes 16801824 | tf_op jit(solution)/shard_map/div | solution.py:162
  478.3 15.2 %collective-permute-done.4 = f32[2,1,1024]{2,0,1:T(2,128)} collective-permute-done((f32[2,1,1024]{2,0,1:T(2,128)}, f32[2,1,1024]{2,0,1:T(2,128)}, u32[]{:S(2)}, u32[]{:S(2)}) %collective-permute-start.4) | collective-permute-done | bytes 8224 | tf_op jit(solution)/shard_map/ppermute | solution.py:45
  499.9 4.0 collective-permute-start.7
  505.8 3.4 pad_maximum_fusion.2
  509.3 13.3 %fusion.93 = f32[2,128,2,64,64]{1,4,3,0,2:T(8,128)} fusion(f32[2,128,2,64,64]{1,3,4,0,2:T(8,128)S(1)} %pad_maximum_fusion.2, f32[1,2,64,64]{2,3,1,0:T(8,128)S(1)} %get-tuple-element.65, f32[1,2,64,64]{2,3,1,0:T(8,128)S(1)} %get-tuple-element.68), kind=kOutput, calls=%fused_computation.155 | convolution fusion | flops 3221241856 | bytes 16842752 | tf_op jit(solution)/shard_map/...rkb,rsbm->...skm/dot_general | solution.py:118
  522.6 5.5 copy.257
  528.1 5.3 copy.258
  533.5 11.3 %fusion.84 = f32[2,128,2,64,64]{1,3,4,0,2:T(8,128)S(1)} fusion(f32[2,128,64,64]{1,3,2,0:T(8,128)} %bitcast.246, f32[1,64,64]{1,2,0:T(8,128)S(1)} %get-tuple-element.73, f32[1,64,64]{1,2,0:T(8,128)S(1)} %get-tuple-element.74), kind=kOutput, calls=%fused_computation.152 | convolution fusion | flops 1610620928 | bytes 12615680 | tf_op jit(solution)/shard_map/...ab,rak->...rkb/dot_general | solution.py:111
  546.5 4.1 pad_maximum_fusion.4
  550.6 15.9 %fusion.99 = f32[2,128,2,64,64]{1,4,3,0,2:T(8,128)S(1)} fusion(f32[2,128,2,64,64]{1,3,4,0,2:T(8,128)} %pad_maximum_fusion.4, f32[1,2,64,64]{2,3,1,0:T(8,128)S(1)} %get-tuple-element.65, f32[1,2,64,64]{2,3,1,0:T(8,128)S(1)} %get-tuple-element.68), kind=kOutput, calls=%fused_computation.157 | convolution fusion | flops 3221241856 | bytes 16842752 | tf_op jit(solution)/shard_map/...rkb,rsbm->...skm/dot_general | solution.py:118
  566.6 4.7 fusion.31
  571.4 10.6 %fusion.102 = f32[2,64,2,128,64]{3,1,4,2,0:T(8,128)S(1)} fusion(f32[2,128,1,64,64]{1,4,3,0,2:T(8,128)} %get-tuple-element.13, f32[2,128,1,64,64]{1,4,3,0,2:T(8,128)} %get-tuple-element.12, f32[1,2,64,64]{2,3,1,0:T(8,128)S(1)} %get-tuple-element.69, f32[1,2,64,64]{2,3,1,0:T(8,128)S(1)} %get-tuple-element.64), kind=kOutput, calls=%fused_computation.158 | convolution fusion | flops 3223339008 | bytes 16842752 | tf_op jit(solution)/shard_map/...skm,srbm->...rkb/dot_general | solution.py:136
  581.9 4.9 copy.374
  589.0 4.9 fusion.65
  596.3 16.1 %copy.267 = f32[2,128,4096]{1,0,2:T(2,128)} copy(f32[2,128,4096]{1,2,0:T(8,128)S(1)} %bitcast.254) | data formatting | bytes 8388608 | tf_op jit(solution)/shard_map/div | solution.py:144
  612.5 5.0 all-to-all-start.4
  617.5 29.9 %broadcast_multiply_fusion.1 = (f32[2,512,1024]{1,2,0:T(8,128)S(1)}, f32[2,512,1024]{1,2,0:T(8,128)}) fusion(f32[512,1024]{0,1:T(8,128)} %copy.209, f32[512,1024]{0,1:T(8,128)} %copy.208, f32[2,512,1024]{1,2,0:T(8,128)} %copy.187, f32[512,1024]{0,1:T(8,128)} %copy.206, f32[512,1024]{0,1:T(8,128)S(1)} %copy.189, f32[512,1024]{0,1:T(8,128)} %copy.205, ...), kind=kLoop, calls=%fused_computation.167 | loop fusion | flops 44040192 | bytes 35700800 | tf_op jit(solution)/shard_map/mul | solution.py:169
  652.3 5.1 collective-permute-start.8
  665.2 5.1 collective-permute-start.11
  675.3 15.0 %broadcast_multiply_fusion = (f32[2,512,1024]{1,2,0:T(8,128)S(1)}, f32[2,512,1024]{1,2,0:T(8,128)}) fusion(f32[512,1024]{0,1:T(8,128)} %copy.216, f32[2,512,1024]{1,2,0:T(8,128)} %get-tuple-element.8, f32[512,1024]{0,1:T(8,128)} %copy.198, f32[2,512,1024]{1,2,0:T(8,128)} %copy-done.3, f32[2,1,1024]{1,2,0:T(8,128)S(1)} %copy.211, f32[2,1,1024]{1,2,0:T(8,128)} %copy.213, ...), kind=kLoop, calls=%fused_computation.166 | loop fusion | flops 16777216 | bytes 20996128 | tf_op jit(solution)/shard_map/mul | solution.py:172
  704.9 4.7 collective-permute-start.15
  711.6 4.5 copy.236
  716.1 5.6 copy.237
  721.6 4.5 copy.268
  726.1 5.4 copy.269
  731.5 5.4 copy.270
  736.9 19.4 %fusion.72 = f32[2,512,1024]{1,2,0:T(8,128)} fusion(f32[2,512,1024]{1,2,0:T(8,128)} %copy.270, f32[2,512,8,128]{1,3,2,0:T(8,128)} %copy.237, f32[2,512,1024]{1,2,0:T(8,128)} %get-tuple-element.6, f32[2,512,1024]{1,2,0:T(8,128)} %copy-done.2, f32[2,1,1024]{1,2,0:T(8,128)S(1)} %copy.218, f32[2,1,1024]{1,2,0:T(8,128)} %copy.220, ...), kind=kLoop, calls=%fused_computation.125 | loop fusion | flops 25165824 | bytes 33579040 | tf_op jit(solution)/shard_map/add | solution.py:208
  756.3 5.4 copy.271
  (118 shorter events, 129.4 us)
Async XLA Ops:
  7.2 94.9 %all-to-all-start = ((f32[2,512,1024]{1,0,2:T(2,128)}), f32[2,512,1024]{1,0,2:T(2,128)}, u32[]{:S(2)}, u32[]{:S(2)}) async-start(f32[2,512,1024]{1,0,2:T(2,128)} %copy.224), calls=%async_computation | async-start | bytes 8388608 | tf_op jit(solution)/shard_map/all_to_all | solution.py:155
  16.4 26.7 %collective-permute-start.18 = (f32[2,128,1024]{2,1,0:T(8,128)}, f32[2,128,1024]{2,1,0:T(8,128)}, u32[]{:S(2)}, u32[]{:S(2)}) collective-permute-start(f32[2,128,1024]{2,1,0:T(8,128)} %get-tuple-element.59), channel_id=1, source_target_pairs={{0,3},{1,2},{2,1},{3,0},{4,7},{5,6},{6,5},{7,4},{8,11},{9,10},{10,... | collective-permute-start | bytes 3145736 | tf_op jit(solution)/shard_map/ppermute | solution.py:30
  18.7 46.7 %collective-permute-start.17 = (f32[2,128,1024]{2,1,0:T(8,128)S(1)}, f32[2,128,1024]{2,1,0:T(8,128)}, u32[]{:S(2)}, u32[]{:S(2)}) collective-permute-start(f32[2,128,1024]{2,1,0:T(8,128)S(1)} %get-tuple-element.57), channel_id=1, source_target_pairs={{0,2},{1,3},{2,0},{3,1},{4,6},{5,7},{6,4},{7,5},{8,10},{9,11},{10,... | collective-permute-start | bytes 3145736 | tf_op jit(solution)/shard_map/ppermute | solution.py:30
  18.9 46.5 %collective-permute-start.16 = (f32[2,128,1024]{2,1,0:T(8,128)S(1)}, f32[2,128,1024]{2,1,0:T(8,128)}, u32[]{:S(2)}, u32[]{:S(2)}) collective-permute-start(f32[2,128,1024]{2,1,0:T(8,128)S(1)} %get-tuple-element.58), channel_id=1, source_target_pairs={{0,1},{1,0},{2,3},{3,2},{4,5},{5,4},{6,7},{7,6},{8,9},{9,8},{10,11... | collective-permute-start | bytes 3145736 | tf_op jit(solution)/shard_map/ppermute | solution.py:30
  127.2 12.8 %copy-start.6 = (f32[64,64]{1,0:T(8,128)S(1)}, f32[64,64]{1,0:T(8,128)}, u32[]{:S(2)}) copy-start(f32[64,64]{1,0:T(8,128)} %copy.223) | copy-start | bytes 49156
  127.2 12.8 %copy-start.8 = (f32[64,64]{1,0:T(8,128)S(1)}, f32[64,64]{1,0:T(8,128)}, u32[]{:S(2)}) copy-start(f32[64,64]{1,0:T(8,128)} %copy.247) | copy-start | bytes 49156
  152.0 27.4 %slice-start.2 = ((s8[8388608]{0:T(1024)(128)(4,1)}), s8[4194304]{0:T(1024)(128)(4,1)S(1)}, s32[]{:S(2)}) async-start(s8[8388608]{0:T(1024)(128)(4,1)} %bitcast.240), calls=%async_computation.7 | async-start | bytes 8388608
  160.4 19.1 %slice-start.3 = ((s8[8388608]{0:T(1024)(128)(4,1)}), s8[4194304]{0:T(1024)(128)(4,1)S(1)}, s32[]{:S(2)}) async-start(s8[8388608]{0:T(1024)(128)(4,1)} %bitcast.240), calls=%async_computation.8 | async-start | bytes 8388608
  216.3 96.4 %all-to-all-start.2 = ((f32[2,4096,128]{2,0,1:T(2,128)}), f32[2,4096,128]{2,0,1:T(2,128)}, u32[]{:S(2)}, u32[]{:S(2)}) async-start(f32[2,4096,128]{2,0,1:T(2,128)} %copy.253), calls=%async_computation.2 | async-start | bytes 8388608 | tf_op jit(solution)/shard_map/all_to_all | solution.py:191
  330.1 65.5 %all-to-all-start.3 = ((f32[2,512,1024]{2,0,1:T(2,128)}), f32[2,512,1024]{2,0,1:T(2,128)}, u32[]{:S(2)}, u32[]{:S(2)}) async-start(f32[2,512,1024]{2,0,1:T(2,128)} %copy.256), calls=%async_computation.3 | async-start | bytes 8388608 | tf_op jit(solution)/shard_map/all_to_all | solution.py:196
  348.8 5.1 copy-start.4
  358.8 2.0 copy-start
  363.7 46.1 %collective-permute-start = (f32[2,1,1024]{2,0,1:T(2,128)S(1)}, f32[2,1,1024]{2,0,1:T(2,128)S(1)}, u32[]{:S(2)}, u32[]{:S(2)}) collective-permute-start(f32[2,1,1024]{2,0,1:T(2,128)S(1)} %copy.190), channel_id=1, source_target_pairs={{4,0},{8,4},{12,8},{16,12},{20,16},{24,20},{28,24},{5,1},{9,5},{13... | collective-permute-start | bytes 24584 | tf_op jit(solution)/shard_map/ppermute | solution.py:45
  367.7 42.4 %collective-permute-start.1 = (f32[2,1,1024]{2,0,1:T(2,128)}, f32[2,1,1024]{2,0,1:T(2,128)}, u32[]{:S(2)}, u32[]{:S(2)}) collective-permute-start(f32[2,1,1024]{2,0,1:T(2,128)} %copy.192), channel_id=1, source_target_pairs={{0,4},{4,8},{8,12},{12,16},{16,20},{20,24},{24,28},{1,5},{5,9},{9,... | collective-permute-start | bytes 24584 | tf_op jit(solution)/shard_map/ppermute | solution.py:43
  395.6 216.9 %all-to-all-start.1 = ((f32[2,4096,128]{2,0,1:T(2,128)}), f32[2,4096,128]{2,0,1:T(2,128)}, u32[]{:S(2)}, u32[]{:S(2)}) async-start(f32[2,4096,128]{2,0,1:T(2,128)} %copy.235), calls=%async_computation.1 | async-start | bytes 8388608 | tf_op jit(solution)/shard_map/all_to_all | solution.py:192
  413.6 17.4 %collective-permute-start.3 = (f32[2,514,1]{1,2,0:T(1,128)}, f32[2,514,1]{1,2,0:T(1,128)S(1)}, u32[]{:S(2)}, u32[]{:S(2)}) collective-permute-start(f32[2,514,1]{1,2,0:T(1,128)} %get-tuple-element.47), channel_id=1, source_target_pairs={{0,1},{1,2},{2,3},{4,5},{5,6},{6,7},{8,9},{9,10},{10,11},{12,13},{... | collective-permute-start | bytes 12344 | tf_op jit(solution)/shard_map/ppermute | solution.py:43
  418.0 13.0 %collective-permute-start.2 = (f32[2,514,1]{1,2,0:T(1,128)}, f32[2,514,1]{1,2,0:T(1,128)S(1)}, u32[]{:S(2)}, u32[]{:S(2)}) collective-permute-start(f32[2,514,1]{1,2,0:T(1,128)} %get-tuple-element.46), channel_id=1, source_target_pairs={{1,0},{2,1},{3,2},{5,4},{6,5},{7,6},{9,8},{10,9},{11,10},{13,12},{... | collective-permute-start | bytes 12344 | tf_op jit(solution)/shard_map/ppermute | solution.py:45
  445.6 2.1 copy-start.1
  451.5 42.0 %collective-permute-start.4 = (f32[2,1,1024]{2,0,1:T(2,128)}, f32[2,1,1024]{2,0,1:T(2,128)}, u32[]{:S(2)}, u32[]{:S(2)}) collective-permute-start(f32[2,1,1024]{2,0,1:T(2,128)} %copy.199), channel_id=1, source_target_pairs={{4,0},{8,4},{12,8},{16,12},{20,16},{24,20},{28,24},{5,1},{9,5},{13... | collective-permute-start | bytes 24584 | tf_op jit(solution)/shard_map/ppermute | solution.py:45
  456.7 39.4 %collective-permute-start.5 = (f32[2,1,1024]{2,0,1:T(2,128)}, f32[2,1,1024]{2,0,1:T(2,128)}, u32[]{:S(2)}, u32[]{:S(2)}) collective-permute-start(f32[2,1,1024]{2,0,1:T(2,128)} %copy.201), channel_id=1, source_target_pairs={{0,4},{4,8},{8,12},{12,16},{16,20},{20,24},{24,28},{1,5},{5,9},{9,... | collective-permute-start | bytes 24584 | tf_op jit(solution)/shard_map/ppermute | solution.py:43
  498.2 7.6 %copy-start.5 = (f32[2,128,1,64,64]{1,3,4,0,2:T(8,128)S(1)}, f32[2,128,1,64,64]{1,3,4,0,2:T(8,128)}, u32[]{:S(2)}) copy-start(f32[2,128,1,64,64]{1,3,4,0,2:T(8,128)} %get-tuple-element.60) | copy-start | bytes 12582916
  499.9 117.6 %collective-permute-start.7 = (f32[2,514,1]{1,2,0:T(1,128)}, f32[2,514,1]{1,2,0:T(1,128)}, u32[]{:S(2)}, u32[]{:S(2)}) collective-permute-start(f32[2,514,1]{1,2,0:T(1,128)} %get-tuple-element.45), channel_id=1, source_target_pairs={{0,1},{1,2},{2,3},{4,5},{5,6},{6,7},{8,9},{9,10},{10,11},{12,13},{... | collective-permute-start | bytes 12344 | tf_op jit(solution)/shard_map/ppermute | solution.py:43
  503.9 113.6 %collective-permute-start.6 = (f32[2,514,1]{1,2,0:T(1,128)}, f32[2,514,1]{1,2,0:T(1,128)}, u32[]{:S(2)}, u32[]{:S(2)}) collective-permute-start(f32[2,514,1]{1,2,0:T(1,128)} %get-tuple-element.44), channel_id=1, source_target_pairs={{1,0},{2,1},{3,2},{5,4},{6,5},{7,6},{9,8},{10,9},{11,10},{13,12},{... | collective-permute-start | bytes 12344 | tf_op jit(solution)/shard_map/ppermute | solution.py:45
  546.5 20.1 %slice-start = ((s8[8388608]{0:T(1024)(128)(4,1)}), s8[4194304]{0:T(1024)(128)(4,1)S(1)}, s32[]{:S(2)}) async-start(s8[8388608]{0:T(1024)(128)(4,1)} %bitcast.237), calls=%async_computation.5 | async-start | bytes 8388608
  550.6 16.0 %slice-start.1 = ((s8[8388608]{0:T(1024)(128)(4,1)}), s8[4194304]{0:T(1024)(128)(4,1)S(1)}, s32[]{:S(2)}) async-start(s8[8388608]{0:T(1024)(128)(4,1)} %bitcast.237), calls=%async_computation.6 | async-start | bytes 8388608
  550.6 16.0 %copy-start.7 = (f32[64,64]{1,0:T(8,128)S(1)}, f32[64,64]{1,0:T(8,128)}, u32[]{:S(2)}) copy-start(f32[64,64]{1,0:T(8,128)} %copy.223) | copy-start | bytes 49156
  550.6 16.0 %copy-start.9 = (f32[64,64]{1,0:T(8,128)S(1)}, f32[64,64]{1,0:T(8,128)}, u32[]{:S(2)}) copy-start(f32[64,64]{1,0:T(8,128)} %copy.246) | copy-start | bytes 49156
  612.5 109.2 %all-to-all-start.4 = ((f32[2,128,4096]{1,0,2:T(2,128)}), f32[2,128,4096]{1,0,2:T(2,128)}, u32[]{:S(2)}, u32[]{:S(2)}) async-start(f32[2,128,4096]{1,0,2:T(2,128)} %copy.267), calls=%async_computation.4 | async-start | bytes 8388608 | tf_op jit(solution)/shard_map/all_to_all | solution.py:207
  647.4 1.9 copy-start.3
  652.3 7.4 collective-permute-start.8
  657.7 5.3 collective-permute-start.9
  665.2 9.9 %collective-permute-start.11 = (f32[2,514,1]{1,2,0:T(1,128)S(1)}, f32[2,514,1]{1,2,0:T(1,128)S(1)}, u32[]{:S(2)}, u32[]{:S(2)}) collective-permute-start(f32[2,514,1]{1,2,0:T(1,128)S(1)} %get-tuple-element.43), channel_id=1, source_target_pairs={{0,1},{1,2},{2,3},{4,5},{5,6},{6,7},{8,9},{9,10},{10,11},{12,13},{... | collective-permute-start | bytes 12344 | tf_op jit(solution)/shard_map/ppermute | solution.py:43
  670.3 4.9 collective-permute-start.10
  690.2 1.9 copy-start.2
  695.1 5.6 collective-permute-start.12
  697.4 5.3 collective-permute-start.13
  704.9 32.0 %collective-permute-start.15 = (f32[2,514,1]{1,2,0:T(1,128)S(1)}, f32[2,514,1]{1,2,0:T(1,128)S(1)}, u32[]{:S(2)}, u32[]{:S(2)}) collective-permute-start(f32[2,514,1]{1,2,0:T(1,128)S(1)} %get-tuple-element.41), channel_id=1, source_target_pairs={{0,1},{1,2},{2,3},{4,5},{5,6},{6,7},{8,9},{9,10},{10,11},{12,13},{... | collective-permute-start | bytes 12344 | tf_op jit(solution)/shard_map/ppermute | solution.py:43
  709.6 27.3 %collective-permute-start.14 = (f32[2,514,1]{1,2,0:T(1,128)S(1)}, f32[2,514,1]{1,2,0:T(1,128)S(1)}, u32[]{:S(2)}, u32[]{:S(2)}) collective-permute-start(f32[2,514,1]{1,2,0:T(1,128)S(1)} %get-tuple-element.40), channel_id=1, source_target_pairs={{1,0},{2,1},{3,2},{5,4},{6,5},{7,6},{9,8},{10,9},{11,10},{13,12},{... | collective-permute-start | bytes 12344 | tf_op jit(solution)/shard_map/ppermute | solution.py:45
